TPU v7x, 512 devices: a whole 4x8x8 slice. The times are simulated.
512 devices in a mesh: gx: 32 (over z, x), gy: 16 (over y, core).
Axes of the slice: x: 4, y: 8, z: 8, core: 2. Of those that a mesh axis runs over, the one named last changes fastest.
Arguments:
- density: float32 [4, 128, 256, 128], P(None, 'gx', 'gy'), may hold values from 0 to 12, as said below
- rate_table: float32 [4, 9], replicated, may hold values from 0 to 128, as said below
Outputs:
- propagated: float32 [4, 128, 256, 128], P(None, 'gx', 'gy')
- step_entries: float32 [4, 5], replicated
Inputs may be any that keep to these rules, and one draw needn't show every extreme that they name: `density`: every entry is positive. `rate_table`: all entries positive; entry r of a row is the constant cr of the steps.
All inputs are finite; a program needn't handle non-finite values.
Results may differ from a plain program's by a relative error of at most 0.0006.
Values sent between devices are 32-bit elements; how exact they have to be, the bound alone decides.
A program may use at most 64 MiB of HBM per device.

v0:
```python
import jax
import jax.numpy as jnp
from jax import lax
from jax.sharding import PartitionSpec as P

tau_step = 0.01
taylor_terms = 16
squarings = 4


def padded_2(array, sides, width):
    for axis, dim in sides:
        size, length = (lax.axis_size(axis), array.shape[dim])
        up = [(i, (i + 1) % size) for i in range(size - 1)]
        down = [(j, i) for i, j in up]
        last = lax.slice_in_dim(array, length - width, length, axis=dim)
        initial = lax.slice_in_dim(array, 0, width, axis=dim)
        before = lax.ppermute(last, axis, up)
        after = lax.ppermute(initial, axis, down)
        array = jnp.concatenate([before, array, after], axis=dim)
    return array


def shift_down(vector_field):
    return jnp.concatenate([jnp.zeros_like(vector_field[..., :1]), vector_field[..., :-1]], axis=-1)


def shift_up(vector_field):
    return jnp.concatenate([vector_field[..., 1:], jnp.zeros_like(vector_field[..., :1])], axis=-1)


def generator_apply(padded, first_i, first_j, member_rates):
    row_count = padded.shape[0] - 4
    col_count = padded.shape[1] - 2
    lattice_depth = padded.shape[2]
    amount_i = (first_i + jnp.arange(row_count, dtype=jnp.int32)).astype(jnp.float32)[:, None, None]
    amount_j = (first_j + jnp.arange(col_count, dtype=jnp.int32)).astype(jnp.float32)[None, :, None]
    amount_k = jnp.arange(lattice_depth, dtype=jnp.int32).astype(jnp.float32)[None, None, :]
    ratio_j = amount_j / member_rates[7]
    ratio_k = amount_k / member_rates[8]
    make_u = member_rates[0] / (1.0 + ratio_j * ratio_j)
    make_v = member_rates[2] / (1.0 + ratio_k * ratio_k)
    outflow = make_u + member_rates[1] * amount_i + make_v + member_rates[3] * amount_j
    outflow = (
        outflow
        + 0.5 * member_rates[4] * amount_i * (amount_i - 1.0)
        + (member_rates[5] + member_rates[6]) * amount_k
    )
    centre = padded[2:-2, 1:-1]
    inflow = make_u * padded[1:-3, 1:-1]
    inflow = inflow + member_rates[1] * (amount_i + 1.0) * padded[3:-1, 1:-1]
    inflow = inflow + make_v * padded[2:-2, :-2]
    inflow = inflow + member_rates[3] * (amount_j + 1.0) * padded[2:-2, 2:]
    inflow = inflow + 0.5 * member_rates[4] * (amount_i + 2.0) * (amount_i + 1.0) * shift_down(
        padded[4:, 1:-1]
    )
    inflow = inflow + member_rates[5] * (amount_k + 1.0) * shift_up(padded[:-4, 1:-1])
    inflow = inflow + member_rates[6] * (amount_k + 1.0) * shift_up(centre)
    return inflow - outflow * centre


def matrix_exponential(small):
    scaled = small * (tau_step / 2.0**squarings)
    identity = jnp.eye(3, dtype=jnp.float32)
    series = identity + jnp.zeros_like(scaled)
    for term_index in range(taylor_terms, 0, -1):
        series = (
            identity
            + jnp.einsum("...ab,...bc->...ac", scaled, series, precision=lax.Precision.HIGHEST)
            / term_index
        )
    for square_index in range(squarings):
        series = jnp.einsum("...ab,...bc->...ac", series, series, precision=lax.Precision.HIGHEST)
    return series


def expand(values):
    return values[:, None, None, None]


def member_sum(left, right):
    return jnp.sum(left * right, axis=(1, 2, 3))


def shards(density, rate_table):
    row_count = density.shape[1]
    col_count = density.shape[2]
    first_i = lax.axis_index("gx") * row_count
    first_j = lax.axis_index("gy") * col_count
    batched = jax.vmap(generator_apply, in_axes=(0, None, None, 0))

    def shallow_image(vector_field):
        widened = padded_2(vector_field, (("gy", 2),), 1)
        padded = padded_2(widened, (("gx", 1),), 2)
        return batched(padded, first_i, first_j, rate_table)

    image_one = shallow_image(density)

    def inner_sum(left, right):
        return lax.psum(member_sum(left, right), ("gx", "gy"))

    def norm_of(vector_field):
        return jnp.sqrt(lax.psum(member_sum(vector_field, vector_field), ("gx", "gy")))

    basis_scale = jnp.sqrt(lax.psum(member_sum(density, density), ("gx", "gy")))
    basis_zero = density / expand(basis_scale)
    candidate = image_one / expand(basis_scale)
    entry_00 = inner_sum(basis_zero, candidate)
    candidate = candidate - expand(entry_00) * basis_zero
    entry_10 = norm_of(candidate)
    basis_one = candidate / expand(entry_10)
    candidate = shallow_image(basis_one)
    entry_01 = inner_sum(basis_zero, candidate)
    candidate = candidate - expand(entry_01) * basis_zero
    entry_11 = inner_sum(basis_one, candidate)
    candidate = candidate - expand(entry_11) * basis_one
    entry_21 = norm_of(candidate)
    basis_two = candidate / expand(entry_21)
    zeros = jnp.zeros_like(entry_00)
    small = jnp.stack(
        [
            jnp.stack([entry_00, entry_01, zeros], -1),
            jnp.stack([entry_10, entry_11, zeros], -1),
            jnp.stack([zeros, entry_21, zeros], -1),
        ],
        -2,
    )
    propagator = matrix_exponential(small)
    propagated = expand(basis_scale) * (
        expand(propagator[:, 0, 0]) * basis_zero
        + expand(propagator[:, 1, 0]) * basis_one
        + expand(propagator[:, 2, 0]) * basis_two
    )
    step_entries = tau_step * jnp.stack([entry_00, entry_10, entry_01, entry_11, entry_21], -1)
    return (propagated, step_entries)


def solution(mesh):
    in_specs = (P(None, "gx", "gy", None), P())
    out_specs = (P(None, "gx", "gy", None), P())
    return jax.shard_map(shards, mesh=mesh, in_specs=in_specs, out_specs=out_specs, check_vma=False)
```

profile of v0, /device:TPU:1, one launch (start us, length us, event | category | flops | bytes accessed | tf_op | source)
XLA Modules:
  0.0 624.7 jit_solution(18076800326916863573)
XLA Ops:
  0.6 0.9 fusion.70
  1.6 4.6 collective-permute-start
  6.2 5.5 collective-permute-start.1
  11.8 1.0 multiply_reduce_fusion.5
  12.8 0.3 slice_reduce_fusion.7
  13.4 1.3 collective-permute-start.2
  14.7 1.3 collective-permute-start.3
  16.1 106.7 %psum.42 = f32[4]{0:T(128)S(1)} all-reduce(f32[4]{0:T(128)S(1)} %multiply_reduce_fusion.5), channel_id=1, replica_groups=mesh['gx'=32,'gy'=16] {'gx','gy'}, use_global_device_ids=true, to_apply=%region_1.0 | all-reduce | flops 4 | bytes 32 | tf_op jit(solution)/shard_map/psum | solution.py:105
  123.0 0.4 multiply_reduce_fusion.4
  123.4 95.3 %psum.43 = f32[4]{0:T(128)S(1)} all-reduce(f32[4]{0:T(128)S(1)} %get-tuple-element.20), channel_id=1, replica_groups=mesh['gx'=32,'gy'=16] {'gx','gy'}, use_global_device_ids=true, to_apply=%region_3.0 | all-reduce | flops 4 | bytes 32 | tf_op jit(solution)/shard_map/psum | solution.py:100
  218.7 0.2 multiply_reduce_fusion.3
  218.9 93.6 %psum.44 = f32[4]{0:T(128)S(1)} all-reduce(f32[4]{0:T(128)S(1)} %multiply_reduce_fusion.3), channel_id=1, replica_groups=mesh['gx'=32,'gy'=16] {'gx','gy'}, use_global_device_ids=true, to_apply=%region_5.0 | all-reduce | flops 4 | bytes 32 | tf_op jit(solution)/shard_map/psum | solution.py:103
  312.6 3.9 collective-permute-start.4
  316.5 1.9 collective-permute-start.5
  318.4 3.0 collective-permute-done.5
  321.5 3.6 collective-permute-start.6
  325.2 1.3 collective-permute-start.7
  326.6 0.2 collective-permute-done.6
  326.8 3.7 collective-permute-done.7
  330.6 0.4 multiply_reduce_fusion.2
  330.9 98.8 %psum.45 = f32[4]{0:T(128)S(1)} all-reduce(f32[4]{0:T(128)S(1)} %get-tuple-element.18), channel_id=1, replica_groups=mesh['gx'=32,'gy'=16] {'gx','gy'}, use_global_device_ids=true, to_apply=%region_7.0 | all-reduce | flops 4 | bytes 32 | tf_op jit(solution)/shard_map/psum | solution.py:100
  429.7 0.2 multiply_reduce_fusion.1
  429.9 94.7 %psum.46 = f32[4]{0:T(128)S(1)} all-reduce(f32[4]{0:T(128)S(1)} %multiply_reduce_fusion.1), channel_id=1, replica_groups=mesh['gx'=32,'gy'=16] {'gx','gy'}, use_global_device_ids=true, to_apply=%region_9.0 | all-reduce | flops 4 | bytes 32 | tf_op jit(solution)/shard_map/psum | solution.py:100
  524.6 0.2 multiply_reduce_fusion
  524.8 94.7 %psum.47 = f32[4]{0:T(128)S(1)} all-reduce(f32[4]{0:T(128)S(1)} %multiply_reduce_fusion), channel_id=1, replica_groups=mesh['gx'=32,'gy'=16] {'gx','gy'}, use_global_device_ids=true, to_apply=%region_11.0 | all-reduce | flops 4 | bytes 32 | tf_op jit(solution)/shard_map/psum | solution.py:103
  619.5 0.7 copy.11
  620.4 0.2 fusion.14
  620.6 0.2 fusion.13
  620.8 0.2 fusion.12
  620.9 0.2 fusion.11
  621.1 0.2 fusion.10
  621.3 0.2 fusion.9
  621.4 0.2 fusion.8
  621.6 0.2 fusion.7
  621.8 0.2 fusion.6
  622.0 0.2 fusion.5
  622.1 0.2 fusion.4
  622.3 0.2 fusion.3
  622.5 0.2 fusion.2
  622.6 0.2 fusion.1
  622.8 0.2 fusion
  623.0 0.2 convolution_add_fusion
  623.1 0.2 fusion.71
  623.3 0.2 fusion.72
  623.5 0.2 fusion.73
  623.6 0.2 fusion.74
  623.8 0.1 slice_reduce_fusion.2
  623.9 0.8 add_multiply_fusion
  (41 shorter events, 1.1 us)
Async XLA Ops:
  0.6 12.7 %copy-start = (f32[4,4,16,128]{3,2,1,0:T(8,128)S(1)}, f32[4,4,16,128]{3,2,1,0:T(8,128)}, u32[]{:S(2)}) copy-start(f32[4,4,16,128]{3,2,1,0:T(8,128)} %param.2) | copy-start | bytes 393220
  1.6 11.8 %collective-permute-start = (f32[4,4,1,128]{3,2,1,0:T(1,128)S(1)}, f32[4,4,1,128]{3,2,1,0:T(1,128)S(1)}, u32[]{:S(2)}, u32[]{:S(2)}) collective-permute-start(f32[4,4,1,128]{3,2,1,0:T(1,128)S(1)} %get-tuple-element.28), channel_id=1, source_target_pairs={{0,1},{1,2},{2,3},{3,4},{4,5},{5,6},{6,7},{7,8},{8,9},{9,10},{10,1... | collective-permute-start | bytes 24584 | tf_op jit(solution)/shard_map/ppermute | solution.py:18
  6.2 7.2 %collective-permute-start.1 = (f32[4,4,1,128]{3,2,1,0:T(1,128)S(1)}, f32[4,4,1,128]{3,2,1,0:T(1,128)S(1)}, u32[]{:S(2)}, u32[]{:S(2)}) collective-permute-start(f32[4,4,1,128]{3,2,1,0:T(1,128)S(1)} %get-tuple-element.29), channel_id=1, source_target_pairs={{1,0},{2,1},{3,2},{4,3},{5,4},{6,5},{7,6},{8,7},{9,8},{10,9},{11,1... | collective-permute-start | bytes 24584 | tf_op jit(solution)/shard_map/ppermute | solution.py:19
  11.7 1.0 copy-start.1
  13.4 109.5 %collective-permute-start.2 = (f32[4,2,18,128]{3,2,1,0:T(8,128)S(1)}, f32[4,2,18,128]{3,2,1,0:T(8,128)S(1)}, u32[]{:S(2)}, u32[]{:S(2)}) collective-permute-start(f32[4,2,18,128]{3,2,1,0:T(8,128)S(1)} %get-tuple-element.25), channel_id=1, source_target_pairs={{0,16},{16,32},{32,48},{48,64},{64,80},{80,96},{96,112},{112,128},... | collective-permute-start | bytes 221192 | tf_op jit(solution)/shard_map/ppermute | solution.py:18
  14.7 108.2 %collective-permute-start.3 = (f32[4,2,18,128]{3,2,1,0:T(8,128)S(1)}, f32[4,2,18,128]{3,2,1,0:T(8,128)S(1)}, u32[]{:S(2)}, u32[]{:S(2)}) collective-permute-start(f32[4,2,18,128]{3,2,1,0:T(8,128)S(1)} %get-tuple-element.24), channel_id=1, source_target_pairs={{16,0},{32,16},{48,32},{64,48},{80,64},{96,80},{112,96},{128,112},... | collective-permute-start | bytes 221192 | tf_op jit(solution)/shard_map/ppermute | solution.py:19
  312.6 5.9 collective-permute-start.4
  316.5 5.0 collective-permute-start.5
  321.5 5.3 collective-permute-start.6
  325.2 5.4 collective-permute-start.7
where the time goes:
time: 626 us; the launch traced here: 625 us
  blocking collectives  584 us (93%)
  starting transfers between devices  23.5 us (4%)
  waiting for transfers between devices  7.01 us (1%)
    psum x3, blocking collectives, inner_sum(): return lax.psum(member_sum(left, right), ('gx', 'gy'))  289 us
    psum x2, blocking collectives, norm_of(): lax.psum(member_sum(vector_field, vector_field), ('gx', 'gy'))  188 us
    psum x1, blocking collectives, shards(): basis_scale = jnp.sqrt(lax.psum(member_sum(density, density), ('gx', 'gy')))  107 us
    ppermute x4, starting transfers between devices, padded_2(): before = lax.ppermute(last, axis, up)  13.5 us
  transfers between devices with their start and end apart: 8, of which 3 were waited for; matrix products, arithmetic and copies ran while one was open for 0% of the time, Pallas kernels for 0%

commit v1 on v0

--- a/solution.py
+++ b/solution.py
@@ -102,7 +102,7 @@
     def norm_of(vector_field):
         return jnp.sqrt(lax.psum(member_sum(vector_field, vector_field), ("gx", "gy")))
 
-    basis_scale = jnp.sqrt(lax.psum(member_sum(density, density), ("gx", "gy")))
+    basis_scale = jnp.sqrt(lax.psum(lax.psum(member_sum(density, density), "gx"), "gy"))
     basis_zero = density / expand(basis_scale)
     candidate = image_one / expand(basis_scale)
     entry_00 = inner_sum(basis_zero, candidate)

time: 626 us -> 624 us (level)
    psum x1 -> x2, blocking collectives: 107 us -> 101 us  [the longest x1 63.1 us: shards(): lax.psum(member_sum(density, density), 'gx')]
where the time goes in v1:
time: 624 us; the launch traced here: 623 us
  blocking collectives  584 us (94%)
  starting transfers between devices  21.3 us (3%)
  waiting for transfers between devices  7.01 us (1%)
    psum x3, blocking collectives, inner_sum(): return lax.psum(member_sum(left, right), ('gx', 'gy'))  293 us
    psum x2, blocking collectives, norm_of(): lax.psum(member_sum(vector_field, vector_field), ('gx', 'gy'))  190 us
    psum x1, blocking collectives, shards(): lax.psum(member_sum(density, density), 'gx')  63.1 us
    psum x1, blocking collectives, shards(): lax.psum(lax.psum(member_sum(density, density), 'gx'), 'gy')  38.3 us
  transfers between devices with their start and end apart: 8, of which 3 were waited for; matrix products, arithmetic and copies ran while one was open for 0% of the time, Pallas kernels for 0%

profile of v1, /device:TPU:1, one launch (start us, length us, event | category | flops | bytes accessed | tf_op | source)
XLA Modules:
  0.0 623.2 jit_solution(16141073609000647724)
XLA Ops:
  0.6 0.9 fusion.70
  1.6 4.6 collective-permute-start
  6.2 5.5 collective-permute-start.1
  11.8 1.0 multiply_reduce_fusion.5
  12.8 0.3 slice_reduce_fusion.7
  13.3 63.1 %psum.49 = f32[4]{0:T(128)S(1)} all-reduce(f32[4]{0:T(128)S(1)} %multiply_reduce_fusion.5), channel_id=1, replica_groups=mesh['gx'=32,'gy'=16] {'gx'}, use_global_device_ids=true, to_apply=%region_1.0 | all-reduce | flops 4 | bytes 32 | tf_op jit(solution)/shard_map/psum | solution.py:105
  76.5 1.3 collective-permute-start.2
  77.8 1.3 collective-permute-start.3
  79.2 38.3 %psum.50 = f32[4]{0:T(128)S(1)} all-reduce(f32[4]{0:T(128)S(1)} %psum.49), channel_id=1, replica_groups=mesh['gx'=32,'gy'=16] {'gy'}, use_global_device_ids=true, to_apply=%region_2.0 | all-reduce | flops 4 | bytes 32 | tf_op jit(solution)/shard_map/psum | solution.py:105
  117.6 0.4 multiply_reduce_fusion.4
  118.0 97.8 %psum.51 = f32[4]{0:T(128)S(1)} all-reduce(f32[4]{0:T(128)S(1)} %get-tuple-element.20), channel_id=1, replica_groups=mesh['gx'=32,'gy'=16] {'gx','gy'}, use_global_device_ids=true, to_apply=%region_4.0 | all-reduce | flops 4 | bytes 32 | tf_op jit(solution)/shard_map/psum | solution.py:100
  215.8 0.2 multiply_reduce_fusion.3
  216.0 95.5 %psum.52 = f32[4]{0:T(128)S(1)} all-reduce(f32[4]{0:T(128)S(1)} %multiply_reduce_fusion.3), channel_id=1, replica_groups=mesh['gx'=32,'gy'=16] {'gx','gy'}, use_global_device_ids=true, to_apply=%region_6.0 | all-reduce | flops 4 | bytes 32 | tf_op jit(solution)/shard_map/psum | solution.py:103
  311.6 2.5 collective-permute-start.4
  314.1 1.9 collective-permute-start.5
  316.1 3.0 collective-permute-done.5
  319.2 2.9 collective-permute-start.6
  322.1 1.3 collective-permute-start.7
  323.5 0.2 collective-permute-done.6
  323.7 3.7 collective-permute-done.7
  327.5 0.4 multiply_reduce_fusion.2
  327.8 100.3 %psum.53 = f32[4]{0:T(128)S(1)} all-reduce(f32[4]{0:T(128)S(1)} %get-tuple-element.18), channel_id=1, replica_groups=mesh['gx'=32,'gy'=16] {'gx','gy'}, use_global_device_ids=true, to_apply=%region_8.0 | all-reduce | flops 4 | bytes 32 | tf_op jit(solution)/shard_map/psum | solution.py:100
  428.2 0.2 multiply_reduce_fusion.1
  428.4 94.8 %psum.54 = f32[4]{0:T(128)S(1)} all-reduce(f32[4]{0:T(128)S(1)} %multiply_reduce_fusion.1), channel_id=1, replica_groups=mesh['gx'=32,'gy'=16] {'gx','gy'}, use_global_device_ids=true, to_apply=%region_10.0 | all-reduce | flops 4 | bytes 32 | tf_op jit(solution)/shard_map/psum | solution.py:100
  523.2 0.2 multiply_reduce_fusion
  523.4 94.6 %psum.55 = f32[4]{0:T(128)S(1)} all-reduce(f32[4]{0:T(128)S(1)} %multiply_reduce_fusion), channel_id=1, replica_groups=mesh['gx'=32,'gy'=16] {'gx','gy'}, use_global_device_ids=true, to_apply=%region_12.0 | all-reduce | flops 4 | bytes 32 | tf_op jit(solution)/shard_map/psum | solution.py:103
  618.0 0.7 copy.11
  619.0 0.2 fusion.14
  619.1 0.2 fusion.13
  619.3 0.2 fusion.12
  619.5 0.2 fusion.11
  619.6 0.2 fusion.10
  619.8 0.2 fusion.9
  620.0 0.2 fusion.8
  620.1 0.2 fusion.7
  620.3 0.2 fusion.6
  620.5 0.2 fusion.5
  620.6 0.2 fusion.4
  620.8 0.2 fusion.3
  621.0 0.2 fusion.2
  621.1 0.2 fusion.1
  621.3 0.2 fusion
  621.5 0.2 convolution_add_fusion
  621.6 0.2 fusion.71
  621.8 0.2 fusion.72
  622.0 0.2 fusion.73
  622.1 0.2 fusion.74
  622.4 0.8 add_multiply_fusion
  (42 shorter events, 1.2 us)
Async XLA Ops:
  0.6 75.8 %copy-start = (f32[4,4,16,128]{3,2,1,0:T(8,128)S(1)}, f32[4,4,16,128]{3,2,1,0:T(8,128)}, u32[]{:S(2)}) copy-start(f32[4,4,16,128]{3,2,1,0:T(8,128)} %param.2) | copy-start | bytes 393220
  1.6 74.9 %collective-permute-start = (f32[4,4,1,128]{3,2,1,0:T(1,128)S(1)}, f32[4,4,1,128]{3,2,1,0:T(1,128)S(1)}, u32[]{:S(2)}, u32[]{:S(2)}) collective-permute-start(f32[4,4,1,128]{3,2,1,0:T(1,128)S(1)} %get-tuple-element.28), channel_id=1, source_target_pairs={{0,1},{1,2},{2,3},{3,4},{4,5},{5,6},{6,7},{7,8},{8,9},{9,10},{10,1... | collective-permute-start | bytes 24584 | tf_op jit(solution)/shard_map/ppermute | solution.py:18
  6.2 70.3 %collective-permute-start.1 = (f32[4,4,1,128]{3,2,1,0:T(1,128)S(1)}, f32[4,4,1,128]{3,2,1,0:T(1,128)S(1)}, u32[]{:S(2)}, u32[]{:S(2)}) collective-permute-start(f32[4,4,1,128]{3,2,1,0:T(1,128)S(1)} %get-tuple-element.29), channel_id=1, source_target_pairs={{1,0},{2,1},{3,2},{4,3},{5,4},{6,5},{7,6},{8,7},{9,8},{10,9},{11,1... | collective-permute-start | bytes 24584 | tf_op jit(solution)/shard_map/ppermute | solution.py:19
  11.7 1.0 copy-start.1
  76.5 41.1 %collective-permute-start.2 = (f32[4,2,18,128]{3,2,1,0:T(8,128)S(1)}, f32[4,2,18,128]{3,2,1,0:T(8,128)S(1)}, u32[]{:S(2)}, u32[]{:S(2)}) collective-permute-start(f32[4,2,18,128]{3,2,1,0:T(8,128)S(1)} %get-tuple-element.25), channel_id=1, source_target_pairs={{0,16},{16,32},{32,48},{48,64},{64,80},{80,96},{96,112},{112,128},... | collective-permute-start | bytes 221192 | tf_op jit(solution)/shard_map/ppermute | solution.py:18
  77.8 39.8 %collective-permute-start.3 = (f32[4,2,18,128]{3,2,1,0:T(8,128)S(1)}, f32[4,2,18,128]{3,2,1,0:T(8,128)S(1)}, u32[]{:S(2)}, u32[]{:S(2)}) collective-permute-start(f32[4,2,18,128]{3,2,1,0:T(8,128)S(1)} %get-tuple-element.24), channel_id=1, source_target_pairs={{16,0},{32,16},{48,32},{64,48},{80,64},{96,80},{112,96},{128,112},... | collective-permute-start | bytes 221192 | tf_op jit(solution)/shard_map/ppermute | solution.py:19
  311.6 4.5 collective-permute-start.4
  314.1 5.0 collective-permute-start.5
  319.2 4.6 collective-permute-start.6
  322.1 5.4 collective-permute-start.7
